TPU v7x, 32 devices: a whole 2x2x4 slice. The times are simulated.
32 devices in a mesh: cell: 8 (over z, y), tm: 4 (over x, core).
Axes of the slice: x: 2, y: 2, z: 4, core: 2. Of those that a mesh axis runs over, the one named last changes fastest.
Arguments:
- snapshots: float32 [384, 5, 6144], P('tm', None, 'cell'), may hold values from -6 to 6
- volumes: float32 [6144], P('cell'), may hold values from 0.1 to 10
- freq_index: int32 [8], replicated, may hold values from 1 to 63, as said below
- block_start: int32 [5], replicated, may hold values from 0 to 256, as said below
Outputs:
- modes: float32 [8, 10, 5, 6144], P('tm', None, None, 'cell')
- triangle: float32 [8, 10, 10], P('tm')
Inputs may be any that keep to these rules, and one draw needn't show every extreme that they name: `freq_index`: distinct indices; the smallest and the largest allowed value both occur. `block_start`: rising; the first is 0 and the last is 256; with s = 64, start b lies within s // 4 of b * s.
All inputs are finite; a program needn't handle non-finite values.
Results may differ from a plain program's by a relative error of at most 0.000078.
Values sent between devices are 32-bit elements; how exact they have to be, the bound alone decides.
A program may use at most 64 MiB of HBM per device.

v0:
```python
import jax
import jax.numpy as jnp
from jax import lax
from jax.sharding import PartitionSpec as P

NFFT = 128
NF = 8
NB = 5


def partner_2(block, axis, distance):
    count = lax.axis_size(axis)
    route = []
    for low in range(count):
        high = low | 1 << distance
        if high != low and high < count:
            route += [(low, high), (high, low)]
    return lax.ppermute(block, axis, route)


def make_table(freq_index, block_start, times):
    tau = times[None, :] - block_start[:, None]
    valid = (tau >= 0) & (tau < NFFT)
    tauf = tau.astype(jnp.float32)
    hann = jnp.where(valid, 0.5 - 0.5 * jnp.cos(2.0 * jnp.pi * tauf / NFFT), 0.0)
    phase = jnp.mod(freq_index[:, None, None] * tau[None, :, :], NFFT).astype(jnp.float32)
    angle = 2.0 * jnp.pi * phase / NFFT
    real_part = hann[None] * jnp.cos(angle)
    imag_part = -hann[None] * jnp.sin(angle)
    table = jnp.stack([real_part, imag_part], axis=1)
    return table.reshape(NF * 2 * NB, times.shape[0])


def outer_sum(lower_a, lower_b):
    first = jnp.einsum("frk,fsk->frs", lower_a, lower_a, precision=lax.Precision.HIGHEST)
    second = jnp.einsum("frk,fsk->frs", lower_b, lower_b, precision=lax.Precision.HIGHEST)
    return first + second


def on_device(snapshots, volumes, freq_index, block_start):
    tdev, nvar, cells = snapshots.shape
    tm_count = lax.axis_size("tm")
    cell_count = lax.axis_size("cell")
    fdev = NF // tm_count
    columns = 2 * NB
    regrouped = lax.all_to_all(snapshots, "tm", split_axis=2, concat_axis=0, tiled=True)
    total_time = regrouped.shape[0]
    quarter = regrouped.shape[2]
    times = jnp.arange(total_time, dtype=jnp.int32)
    table = make_table(freq_index, block_start, times)
    flat = regrouped.reshape(total_time, nvar * quarter)
    local_spec = jnp.dot(
        table, flat, precision=lax.Precision.HIGHEST, preferred_element_type=jnp.float32
    )
    local_spec = local_spec.reshape(NF * columns, nvar, quarter)
    spectra = lax.all_to_all(local_spec, "tm", split_axis=0, concat_axis=2, tiled=True)
    spectra = spectra.reshape(fdev, columns, nvar, cells)
    weighted = spectra * jnp.sqrt(volumes)[None, None, None, :]
    weighted = weighted.reshape(fdev, columns, nvar * cells)
    gram_local = jnp.einsum("frc,fsc->frs", weighted, weighted, precision=lax.Precision.HIGHEST)
    lower = jnp.linalg.cholesky(gram_local)
    for bit in range(cell_count.bit_length() - 1):
        partner = partner_2(lower, "cell", bit)
        lower = jnp.linalg.cholesky(outer_sum(lower, partner))
    solved = jax.vmap(lambda a, b: jax.scipy.linalg.solve_triangular(a, b, lower=True))(
        lower, weighted
    )
    total_rows = nvar * cells * cell_count
    modes = (jnp.sqrt(jnp.float32(total_rows)) * solved).reshape(fdev, columns, nvar, cells)
    triangle = jnp.transpose(lower, (0, 2, 1)) / jnp.sqrt(jnp.float32(total_rows * NFFT))
    return (modes, triangle)


def solution(mesh):
    placed = (P("tm", None, "cell"), P("cell"), P(), P())
    return jax.shard_map(
        on_device,
        mesh=mesh,
        in_specs=placed,
        out_specs=(P("tm", None, None, "cell"), P("tm", None, None)),
        check_vma=False,
    )
```

profile of v0, /device:TPU:0, one launch (start us, length us, event | category | flops | bytes accessed | tf_op | source)
XLA Modules:
  0.0 86.6 jit_solution(418395447289568936)
XLA Ops:
  0.6 2.3 %copy.56 = f32[96,5,768]{0,1,2:T(8,128)S(1)} copy(f32[96,5,768]{2,0,1:T(8,128)} %param.5) | data formatting | bytes 2949120 | tf_op args[0]
  3.0 3.5 %reshape.153 = f32[4,1,92160]{2,1,0:T(1,128)} reshape(f32[768,5,96]{2,1,0:T(8,128)S(1)} %bitcast.52) | data formatting | bytes 2949120
  6.4 4.3 %all-to-all-start = ((f32[4,1,92160]{2,1,0:T(1,128)}), f32[4,1,92160]{2,1,0:T(1,128)S(1)}, u32[]{:S(2)}, u32[]{:S(2)}) async-start(f32[4,1,92160]{2,1,0:T(1,128)} %reshape.153), calls=%async_computation | async-start | bytes 2949120 | tf_op jit(solution)/shard_map/all_to_all | solution.py:46
  10.8 0.1 subtract_select_fusion
  11.0 0.5 cosine_multiply_fusion
  11.5 18.3 %all-to-all-done = f32[4,1,92160]{2,1,0:T(1,128)S(1)} async-done(((f32[4,1,92160]{2,1,0:T(1,128)}), f32[4,1,92160]{2,1,0:T(1,128)S(1)}, u32[]{:S(2)}, u32[]{:S(2)}) %all-to-all-start) | async-done | bytes 1474592 | tf_op jit(solution)/shard_map/all_to_all | solution.py:46
  29.8 0.5 broadcast.245
  30.3 6.1 %reduce.4 = f32[4,92160]{1,0:T(4,128)} reduce(f32[4,1,92160]{2,1,0:T(1,128)S(1)} %all-to-all-done, f32[]{:T(128)} %broadcast.245), dimensions={1}, to_apply=%all_to_all.22.reduce_sub_computation | reduce | bytes 2949124 | tf_op jit(solution)/shard_map/all_to_all | solution.py:46
  36.4 3.0 %reshape.154 = f32[768,5,96]{2,1,0:T(8,128)S(1)} reshape(f32[4,92160]{1,0:T(4,128)} %reduce.4) | data formatting | bytes 2949120
  39.4 2.6 %copy.57 = f32[4,96,5,192]{1,0,3,2:T(4,128)} copy(f32[4,96,5,192]{1,2,3,0:T(8,128)S(1)} %bitcast.51) | data formatting | bytes 2949120 | tf_op jit(solution)/shard_map/all_to_all | solution.py:46
  41.9 2.3 %reshape.147 = f32[384,960]{0,1:T(8,128)S(1)} reshape(f32[4,96,5,192]{1,0,3,2:T(4,128)} %copy.57) | data formatting | bytes 2949120 | tf_op jit(solution)/shard_map/reshape | solution.py:51
  44.2 2.0 %fusion.17 = f32[80,5,192]{2,0,1:T(8,128)S(1)} fusion(f32[80,384,1]{1,0,2:T(8,128)S(1)} %reshape.150, f32[5,192,384]{2,1,0:T(8,128)S(1)} %bitcast.53), kind=kOutput, calls=%fused_computation.51 | convolution fusion | flops 353894400 | bytes 1904640 | tf_op jit(solution)/shard_map/dot_general | solution.py:52
  46.3 0.3 copy.58
  46.5 1.2 %reshape.155 = f32[4,1,19200]{2,1,0:T(1,128)} reshape(f32[80,5,192]{2,1,0:T(8,128)S(1)} %copy.58) | data formatting | bytes 614400
  47.7 3.6 %all-to-all-start.1 = ((f32[4,1,19200]{2,1,0:T(1,128)}), f32[4,1,19200]{2,1,0:T(1,128)S(1)}, u32[]{:S(2)}, u32[]{:S(2)}) async-start(f32[4,1,19200]{2,1,0:T(1,128)} %reshape.155), calls=%async_computation.1 | async-start | bytes 614400 | tf_op jit(solution)/shard_map/all_to_all | solution.py:56
  51.4 6.2 %all-to-all-done.1 = f32[4,1,19200]{2,1,0:T(1,128)S(1)} async-done(((f32[4,1,19200]{2,1,0:T(1,128)}), f32[4,1,19200]{2,1,0:T(1,128)S(1)}, u32[]{:S(2)}, u32[]{:S(2)}) %all-to-all-start.1) | async-done | bytes 307232 | tf_op jit(solution)/shard_map/all_to_all | solution.py:56
  57.6 1.5 %reduce.5 = f32[4,19200]{1,0:T(4,128)S(1)} reduce(f32[4,1,19200]{2,1,0:T(1,128)S(1)} %all-to-all-done.1, f32[]{:T(128)} %broadcast.245), dimensions={1}, to_apply=%all_to_all.25.reduce_sub_computation | reduce | bytes 614404 | tf_op jit(solution)/shard_map/all_to_all | solution.py:56
  59.1 0.3 reshape.156
  59.5 0.3 copy.60
  59.7 0.3 reshape.148
  60.0 0.9 %fusion.1 = f32[2,10,10]{2,1,0:T(8,128)S(1)} fusion(f32[2,10,3840]{2,1,0:T(8,128)S(1)} %reshape.148, f32[3840]{0:T(1024)S(1)} %mul.98), kind=kOutput, calls=%fused_computation.5 | convolution fusion | flops 9292800 | bytes 323360 | tf_op jit(solution)/shard_map/frc,fsc->frs/dot_general | solution.py:60
  61.0 1.8 %custom-call.11 = f32[2,10,10]{2,1,0:T(8,128)S(1)} custom-call(f32[2,10,10]{2,1,0:T(8,128)S(1)} %fusion.12), custom_call_target="Cholesky" | custom-call | tf_op jit(solution)/shard_map/jit(cholesky)/cholesky | solution.py:61
  62.9 0.1 compare_reduce_fusion.3
  63.1 2.3 %collective-permute-start = (f32[2,10,10]{2,1,0:T(8,128)S(1)}, f32[2,10,10]{2,1,0:T(8,128)S(1)}, u32[]{:S(2)}, u32[]{:S(2)}) collective-permute-start(f32[2,10,10]{2,1,0:T(8,128)S(1)} %select_select_fusion.3), channel_id=1, source_target_pairs={{0,4},{4,0},{8,12},{12,8},{16,20},{20,16},{24,28},{28,24},{1,5},{5... | collective-permute-start | bytes 2408 | tf_op jit(solution)/shard_map/ppermute | solution.py:18
  65.4 0.1 fusion.18
  65.5 1.6 %collective-permute-done = f32[2,10,10]{2,1,0:T(8,128)S(1)} collective-permute-done((f32[2,10,10]{2,1,0:T(8,128)S(1)}, f32[2,10,10]{2,1,0:T(8,128)S(1)}, u32[]{:S(2)}, u32[]{:S(2)}) %collective-permute-start) | collective-permute-done | bytes 832 | tf_op jit(solution)/shard_map/ppermute | solution.py:18
  67.1 0.1 convolution_add_fusion.2
  67.2 0.1 copy.64
  67.4 1.8 %custom-call.12 = f32[2,10,10]{2,1,0:T(8,128)S(1)} custom-call(f32[2,10,10]{2,1,0:T(8,128)S(1)} %fusion.11), custom_call_target="Cholesky" | custom-call | tf_op jit(solution)/shard_map/jit(cholesky)/cholesky | solution.py:64
  69.2 0.1 compare_reduce_fusion.2
  69.4 2.1 %collective-permute-start.1 = (f32[2,10,10]{2,1,0:T(8,128)S(1)}, f32[2,10,10]{2,1,0:T(8,128)S(1)}, u32[]{:S(2)}, u32[]{:S(2)}) collective-permute-start(f32[2,10,10]{2,1,0:T(8,128)S(1)} %select_select_fusion.2), channel_id=1, source_target_pairs={{0,8},{8,0},{4,12},{12,4},{16,24},{24,16},{20,28},{28,20},{1,9},{9... | collective-permute-start | bytes 2408 | tf_op jit(solution)/shard_map/ppermute | solution.py:18
  71.5 0.1 fusion.19
  71.7 1.6 %collective-permute-done.1 = f32[2,10,10]{2,1,0:T(8,128)S(1)} collective-permute-done((f32[2,10,10]{2,1,0:T(8,128)S(1)}, f32[2,10,10]{2,1,0:T(8,128)S(1)}, u32[]{:S(2)}, u32[]{:S(2)}) %collective-permute-start.1) | collective-permute-done | bytes 832 | tf_op jit(solution)/shard_map/ppermute | solution.py:18
  73.2 0.1 convolution_add_fusion.1
  73.4 0.1 copy.67
  73.5 1.8 %custom-call.13 = f32[2,10,10]{2,1,0:T(8,128)S(1)} custom-call(f32[2,10,10]{2,1,0:T(8,128)S(1)} %fusion.10), custom_call_target="Cholesky" | custom-call | tf_op jit(solution)/shard_map/jit(cholesky)/cholesky | solution.py:64
  75.4 0.1 compare_reduce_fusion.1
  75.6 3.0 %collective-permute-start.2 = (f32[2,10,10]{2,1,0:T(8,128)S(1)}, f32[2,10,10]{2,1,0:T(8,128)S(1)}, u32[]{:S(2)}, u32[]{:S(2)}) collective-permute-start(f32[2,10,10]{2,1,0:T(8,128)S(1)} %select_select_fusion.1), channel_id=1, source_target_pairs={{0,16},{16,0},{4,20},{20,4},{8,24},{24,8},{12,28},{28,12},{1,17},{... | collective-permute-start | bytes 2408 | tf_op jit(solution)/shard_map/ppermute | solution.py:18
  78.6 0.1 fusion.20
  78.7 1.6 %collective-permute-done.2 = f32[2,10,10]{2,1,0:T(8,128)S(1)} collective-permute-done((f32[2,10,10]{2,1,0:T(8,128)S(1)}, f32[2,10,10]{2,1,0:T(8,128)S(1)}, u32[]{:S(2)}, u32[]{:S(2)}) %collective-permute-start.2) | collective-permute-done | bytes 832 | tf_op jit(solution)/shard_map/ppermute | solution.py:18
  80.3 0.1 convolution_add_fusion
  80.6 1.8 %custom-call.14 = f32[2,10,10]{2,1,0:T(8,128)S(1)} custom-call(f32[2,10,10]{2,1,0:T(8,128)S(1)} %fusion.9), custom_call_target="Cholesky" | custom-call | tf_op jit(solution)/shard_map/jit(cholesky)/cholesky | solution.py:64
  82.4 0.1 compare_reduce_fusion
  82.6 1.5 %custom-call.7 = f32[2,1,10,10]{2,3,1,0:T(8,128)S(1)} custom-call(f32[2,1,10,10]{3,2,1,0:T(8,128)S(1)} %get-tuple-element.12), custom_call_target="InvertDiagBlocksLowerTriangular" | custom-call | tf_op jit(solution)/shard_map/vmap(jit(_solve_triangular))/triangular_solve | solution.py:65
  84.2 0.6 convolution_multiply_fusion
  84.8 0.1 reshape.152
  85.0 1.0 %copy.73 = f32[2,10,5,768]{3,0,2,1:T(2,128)} copy(f32[2,10,5,768]{3,2,1,0:T(8,128)S(1)} %reshape.152) | data formatting | bytes 614400
  85.9 0.7 copy.74
  (28 shorter events, 1.0 us)
Async XLA Ops:
  6.4 4.3 %copy-start.1 = (s32[5]{0:T(128)S(1)}, s32[5]{0:T(128)}, u32[]{:S(2)}) copy-start(s32[5]{0:T(128)} %param.8) | copy-start | bytes 64
  6.4 4.6 %copy-start.2 = (s32[8]{0:T(128)S(1)}, s32[8]{0:T(128)}, u32[]{:S(2)}) copy-start(s32[8]{0:T(128)} %param.7) | copy-start | bytes 100
  6.4 23.4 %all-to-all-start = ((f32[4,1,92160]{2,1,0:T(1,128)}), f32[4,1,92160]{2,1,0:T(1,128)S(1)}, u32[]{:S(2)}, u32[]{:S(2)}) async-start(f32[4,1,92160]{2,1,0:T(1,128)} %reshape.153), calls=%async_computation | async-start | bytes 2949120 | tf_op jit(solution)/shard_map/all_to_all | solution.py:46
  46.3 5.1 %copy-start = (f32[768]{0:T(1024)S(1)}, f32[768]{0:T(1024)}, u32[]{:S(2)}) copy-start(f32[768]{0:T(1024)} %param.6) | copy-start | bytes 9220
  47.7 9.9 %all-to-all-start.1 = ((f32[4,1,19200]{2,1,0:T(1,128)}), f32[4,1,19200]{2,1,0:T(1,128)S(1)}, u32[]{:S(2)}, u32[]{:S(2)}) async-start(f32[4,1,19200]{2,1,0:T(1,128)} %reshape.155), calls=%async_computation.1 | async-start | bytes 614400 | tf_op jit(solution)/shard_map/all_to_all | solution.py:56
  63.1 4.0 %collective-permute-start = (f32[2,10,10]{2,1,0:T(8,128)S(1)}, f32[2,10,10]{2,1,0:T(8,128)S(1)}, u32[]{:S(2)}, u32[]{:S(2)}) collective-permute-start(f32[2,10,10]{2,1,0:T(8,128)S(1)} %select_select_fusion.3), channel_id=1, source_target_pairs={{0,4},{4,0},{8,12},{12,8},{16,20},{20,16},{24,28},{28,24},{1,5},{5... | collective-permute-start | bytes 2408 | tf_op jit(solution)/shard_map/ppermute | solution.py:18
  69.4 3.8 %collective-permute-start.1 = (f32[2,10,10]{2,1,0:T(8,128)S(1)}, f32[2,10,10]{2,1,0:T(8,128)S(1)}, u32[]{:S(2)}, u32[]{:S(2)}) collective-permute-start(f32[2,10,10]{2,1,0:T(8,128)S(1)} %select_select_fusion.2), channel_id=1, source_target_pairs={{0,8},{8,0},{4,12},{12,4},{16,24},{24,16},{20,28},{28,20},{1,9},{9... | collective-permute-start | bytes 2408 | tf_op jit(solution)/shard_map/ppermute | solution.py:18
  75.6 4.8 %collective-permute-start.2 = (f32[2,10,10]{2,1,0:T(8,128)S(1)}, f32[2,10,10]{2,1,0:T(8,128)S(1)}, u32[]{:S(2)}, u32[]{:S(2)}) collective-permute-start(f32[2,10,10]{2,1,0:T(8,128)S(1)} %select_select_fusion.1), channel_id=1, source_target_pairs={{0,16},{16,0},{4,20},{20,4},{8,24},{24,8},{12,28},{28,12},{1,17},{... | collective-permute-start | bytes 2408 | tf_op jit(solution)/shard_map/ppermute | solution.py:18
where the time goes:
time: 87 us; the launch traced here: 86.6 us
  waiting for transfers between devices  29.2 us (34%)
  local copies, waits for them, and re-layouts  18.6 us (21%)
  other arithmetic  18.1 us (21%)
  starting transfers between devices  15.4 us (18%)
  matrix products  4.37 us (5%)
  between operations  0.87 us (1%)
    all_to_all x1, waiting for transfers between devices, on_device(): lax.all_to_all(snapshots, 'tm', split_axis=2, concat_axis=0, tiled=True)  18.3 us
    unnamed x13, local copies, waits for them, and re-layouts  11.9 us
    ppermute x3, starting transfers between devices, partner_2(): return lax.ppermute(block, axis, route)  7.44 us
    all_to_all x1, waiting for transfers between devices, on_device(): lax.all_to_all(local_spec, 'tm', split_axis=0, concat_axis=2, tiled=True)  6.23 us
    all_to_all x1, other arithmetic, on_device(): lax.all_to_all(snapshots, 'tm', split_axis=2, concat_axis=0, tiled=True)  6.05 us
    another operation x10, other arithmetic, on_device(): lower = jnp.linalg.cholesky(outer_sum(lower, partner))  5.95 us
    ppermute x3, waiting for transfers between devices, partner_2(): return lax.ppermute(block, axis, route)  4.74 us
    all_to_all x1, starting transfers between devices, on_device(): lax.all_to_all(snapshots, 'tm', split_axis=2, concat_axis=0, tiled=True)  4.34 us
  transfers between devices with their start and end apart: 5, of which 5 were waited for; matrix products, arithmetic and copies ran while one was open for 1% of the time, Pallas kernels for 0%

commit v1 on v0

v1 whole, which is shorter than its diff:
```python
import functools

import jax
import jax.numpy as jnp
from jax import lax
from jax.experimental import pallas as pl
from jax.experimental.pallas import tpu as pltpu
from jax.sharding import PartitionSpec as P

NFFT = 128
MESH = pl.DeviceIdType.MESH
F32 = jnp.float32
BF16 = jnp.bfloat16
NT = (((1,), (1,)), ((), ()))
ROWS = 32


def split3(a):
    high = a.astype(BF16)
    rest = a - high.astype(F32)
    middle = rest.astype(BF16)
    low = (rest - middle.astype(F32)).astype(BF16)
    return high, middle, low


def exact_dot(a, b, dims=(((1,), (0,)), ((), ()))):
    return lax.dot_general(
        a, b, dims, precision=lax.Precision.HIGHEST, preferred_element_type=F32
    )


def kernel(
    sizes,
    x_ref,
    vol_ref,
    freq_ref,
    start_ref,
    modes_ref,
    tri_ref,
    snap,
    part,
    got,
    wcat,
    grams,
    local_sem,
    xsend_sem,
    xrecv_sem,
    psend_sem,
    precv_sem,
    gsend_sem,
    grecv_sem,
):
    cell_count, tdev, nvar, cells, nf, nb = sizes
    fdev = nf // 4
    kept = nb - 1
    half = cells // 2
    span = 2 * tdev
    per = kept * 2 * fdev
    rows = nf * 2 * kept
    cell = lax.axis_index("cell")
    tm = lax.axis_index("tm")
    group, core = tm // 2, lax.rem(tm, 2)
    partner = group * 2 + 1 - core
    targets = ((1 - group) * 2 + core, (1 - group) * 2 + 1 - core, partner)

    my_rows = pl.ds(pl.multiple_of(core * tdev, 8), tdev)
    my_cells = pl.ds(pl.multiple_of(core * half, 128), half)
    other_cells = pl.ds(pl.multiple_of((1 - core) * half, 128), half)

    local = []
    for v in range(nvar):
        copy = pltpu.make_async_copy(
            x_ref.at[v, :, my_cells], snap.at[v, my_rows, :], local_sem.at[v]
        )
        copy.start()
        local.append(copy)

    barrier = pltpu.get_barrier_semaphore()
    for target in targets:
        pl.semaphore_signal(barrier, inc=1, device_id={"tm": target}, device_id_type=MESH)
    for step in range(1, cell_count):
        pl.semaphore_signal(
            barrier,
            inc=1,
            device_id={"cell": lax.rem(cell + step, cell_count)},
            device_id_type=MESH,
        )

    row = lax.broadcasted_iota(jnp.int32, (rows, span), 0)
    time = lax.broadcasted_iota(jnp.int32, (rows, span), 1) + group * span
    imag = row % 2
    row_block = (row // (2 * fdev)) % kept
    row_freq = (row // per) * fdev + (row // 2) % fdev
    start = jnp.zeros((rows, span), jnp.int32)
    for b in range(kept):
        start = jnp.where(row_block == b, start_ref[group + b], start)
    freq = jnp.zeros((rows, span), jnp.int32)
    for f in range(nf):
        freq = jnp.where(row_freq == f, freq_ref[f], freq)
    tau = time - start
    valid = (tau >= 0) & (tau < NFFT)
    turn = 2.0 * jnp.pi / NFFT
    hann = jnp.where(valid, 0.5 - 0.5 * jnp.cos((tau & (NFFT - 1)).astype(F32) * turn), 0.0)

    pl.semaphore_wait(barrier, len(targets) + cell_count - 1)

    exchange = []
    for v in range(nvar):
        copy = pltpu.make_async_remote_copy(
            src_ref=x_ref.at[v, :, other_cells],
            dst_ref=snap.at[v, my_rows, :],
            send_sem=xsend_sem.at[v],
            recv_sem=xrecv_sem.at[v],
            device_id={"tm": partner},
            device_id_type=MESH,
        )
        copy.start()
        exchange.append(copy)

    phase = (freq * tau + imag * (NFFT // 4)) & (NFFT - 1)
    table = hann * jnp.cos(phase.astype(F32) * turn)
    th, tmid, tl = split3(table)
    table3 = jnp.concatenate([th, tmid, tl], axis=0)

    sends = []
    for v in range(nvar):
        local[v].wait()
        exchange[v].wait_recv()
        sh, sm, sl = split3(snap[v])
        a = jnp.dot(table3, sh, preferred_element_type=F32)
        b = jnp.dot(table3[: 2 * rows], sm, preferred_element_type=F32)
        c = jnp.dot(th, sl, preferred_element_type=F32)
        small = a[2 * rows :] + b[rows:] + c
        part[v] = a[:rows] + ((a[rows : 2 * rows] + b[:rows]) + small)
        for k, target in enumerate(targets):
            copy = pltpu.make_async_remote_copy(
                src_ref=part.at[v, pl.ds(pl.multiple_of(target * per, 8), per), :],
                dst_ref=got.at[group, v, :, my_cells],
                send_sem=psend_sem.at[k, v],
                recv_sem=precv_sem.at[k, v],
                device_id={"tm": target},
                device_id_type=MESH,
            )
            copy.start()
            sends.append((v, copy))
        got[group, v, :, my_cells] = part[v, pl.ds(pl.multiple_of(tm * per, 8), per), :]

    root = jnp.sqrt(vol_ref[...])
    gram = jnp.zeros((3 * ROWS, 128), F32)
    for v in range(nvar):
        for w, copy in sends:
            if w == v:
                copy.wait_recv()
        pad = jnp.zeros((ROWS - per, cells), F32)
        first = jnp.concatenate([got[0, v], pad], axis=0)
        second = pltpu.roll(jnp.concatenate([got[1, v], pad], axis=0), 2 * fdev, 0)
        weighted = (first + second) * root
        wh, wm, wl = split3(weighted)
        wcat[v] = jnp.concatenate([wh, wm, wl, wh, wm, wh], axis=0)
        lhs = jnp.concatenate([wh, wm, wl], axis=0)
        rhs = jnp.concatenate([wh, wm, wl, jnp.zeros_like(wh)], axis=0)
        gram = gram + lax.dot_general(lhs, rhs, NT, preferred_element_type=F32)

    lane = lax.broadcasted_iota(jnp.int32, (ROWS, 128), 1)
    line = lax.broadcasted_iota(jnp.int32, (ROWS, 128), 0)
    gram = gram[:ROWS] + (gram[ROWS : 2 * ROWS] + gram[2 * ROWS :])
    gram = gram + (pltpu.roll(gram, 128 - ROWS, 1) + pltpu.roll(gram, 128 - 2 * ROWS, 1))
    gram = jnp.where(lane < ROWS, gram, 0.0)
    packed = gram[0:8]
    for q in range(1, ROWS // 8):
        packed = packed + pltpu.roll(gram[8 * q : 8 * q + 8], ROWS * q, 1)
    grams[cell] = packed

    gsends = []
    for step in range(1, cell_count):
        copy = pltpu.make_async_remote_copy(
            src_ref=grams.at[cell],
            dst_ref=grams.at[cell],
            send_sem=gsend_sem.at[step],
            recv_sem=grecv_sem.at[step],
            device_id={"cell": lax.rem(cell + step, cell_count)},
            device_id_type=MESH,
        )
        copy.start()
        gsends.append(copy)
    for copy in gsends:
        copy.wait_recv()
    total = grams[0]
    for q in range(1, cell_count):
        total = total + grams[q]

    pieces = [total] + [pltpu.roll(total, 128 - ROWS * q, 1) for q in range(1, ROWS // 8)]
    full = jnp.concatenate(pieces, axis=0)
    aug = jnp.where(lane < ROWS, full, jnp.where(lane - ROWS == line, 1.0, 0.0))
    columns = 2 * nb
    used = fdev * columns
    line_freq = (line // 2) % fdev
    order = jnp.where(line < used, (line % 2) * nb + line // (2 * fdev), -1)
    for j in range(columns - 1):
        base = (j % nb) * 2 * fdev + j // nb
        pivot = aug[base : base + 1, :]
        where = jnp.full((ROWS, 128), base, jnp.int32)
        for f in range(1, fdev):
            pivot = jnp.where(line_freq == f, aug[base + 2 * f : base + 2 * f + 1, :], pivot)
            where = jnp.where(line_freq == f, base + 2 * f, where)
        hit = lane == where
        column = jnp.sum(jnp.where(hit, aug, 0.0), axis=1, keepdims=True)
        diagonal = jnp.sum(jnp.where(hit, pivot, 0.0), axis=1, keepdims=True)
        factor = jnp.where(order > j, column / diagonal, 0.0)
        aug = aug - factor * pivot
    diagonal = jnp.sum(jnp.where(lane == line, aug, 0.0), axis=1, keepdims=True)
    diagonal = jnp.where(line < used, diagonal, 1.0)
    aug = aug * (1.0 / jnp.sqrt(diagonal))

    total_rows = nvar * cells * cell_count
    out_row = lax.broadcasted_iota(jnp.int32, (ROWS, ROWS), 0)
    in_row = lax.broadcasted_iota(jnp.int32, (ROWS, ROWS), 1)
    place = ((in_row % 2) * nb + in_row // (2 * fdev)) * fdev + (in_row // 2) % fdev
    permute = jnp.where((in_row < used) & (out_row == place), 1.0, 0.0)
    solve = exact_dot(permute, aug) * jnp.sqrt(F32(total_rows))
    solve = jnp.where((lane >= ROWS) & (lane < 2 * ROWS), solve, 0.0)
    solve = solve + pltpu.roll(solve, 2 * ROWS, 1)
    solve = solve + pltpu.roll(solve, ROWS, 1)
    eh, em, el = [e.astype(F32) for e in split3(solve)]
    lhs = jnp.concatenate(
        [
            jnp.where(lane < 3 * ROWS, eh, em),
            jnp.where(lane < ROWS, em, jnp.where(lane < 2 * ROWS, el, 0.0)),
        ],
        axis=1,
    )[:, : 6 * ROWS].astype(BF16)
    for v in range(nvar):
        modes = jnp.dot(lhs, wcat[v], preferred_element_type=F32)
        for j in range(columns):
            modes_ref[j, v, :, :] = modes[j * fdev : (j + 1) * fdev, :]

    tri_row = lax.broadcasted_iota(jnp.int32, (16, ROWS), 0)
    tri_in = lax.broadcasted_iota(jnp.int32, (16, ROWS), 1)
    tri_out = lax.broadcasted_iota(jnp.int32, (16, 128), 0)
    tri_lane = lax.broadcasted_iota(jnp.int32, (16, 128), 1)

    def picks(out, inner, f):
        match = ((inner % 2) * nb + inner // (2 * fdev) == out) & ((inner // 2) % fdev == f)
        return jnp.where(match & (inner < used), 1.0, 0.0)

    tri_scale = F32(1.0) / jnp.sqrt(F32(total_rows * NFFT))
    upper = lax.broadcasted_iota(jnp.int32, (16, 16), 0) <= lax.broadcasted_iota(
        jnp.int32, (16, 16), 1
    )
    for f in range(fdev):
        left = exact_dot(picks(tri_row, tri_in, f), aug)
        both = exact_dot(left, picks(tri_out, tri_lane, f), NT)
        tri = jnp.where(upper, both * tri_scale, 0.0)
        tri_ref[f] = tri[:columns, :columns]

    for copy in exchange:
        copy.wait_send()
    for _, copy in sends:
        copy.wait_send()
    for copy in gsends:
        copy.wait_send()


def on_device(snapshots, volumes, freq_index, block_start):
    tdev, nvar, cells = snapshots.shape
    cell_count = lax.axis_size("cell")
    nf, nb = freq_index.shape[0], block_start.shape[0]
    fdev = nf // lax.axis_size("tm")
    columns = 2 * nb
    kept = nb - 1
    half = cells // 2
    per = kept * 2 * fdev
    sizes = (cell_count, tdev, nvar, cells, nf, nb)
    dma = pltpu.SemaphoreType.DMA
    modes, triangle = pl.pallas_call(
        functools.partial(kernel, sizes),
        out_shape=(
            jax.ShapeDtypeStruct((columns, nvar, fdev, cells), F32),
            jax.ShapeDtypeStruct((fdev, columns, columns), F32),
        ),
        in_specs=[
            pl.BlockSpec(memory_space=pl.ANY),
            pl.BlockSpec(memory_space=pltpu.VMEM),
            pl.BlockSpec(memory_space=pltpu.SMEM),
            pl.BlockSpec(memory_space=pltpu.SMEM),
        ],
        out_specs=(
            pl.BlockSpec(memory_space=pltpu.VMEM),
            pl.BlockSpec(memory_space=pltpu.VMEM),
        ),
        scratch_shapes=[
            pltpu.VMEM((nvar, 2 * tdev, half), F32),
            pltpu.VMEM((nvar, nf * 2 * kept, half), F32),
            pltpu.VMEM((2, nvar, per, cells), F32),
            pltpu.VMEM((nvar, 6 * ROWS, cells), BF16),
            pltpu.VMEM((cell_count, 8, 128), F32),
            dma((nvar,)),
            dma((nvar,)),
            dma((nvar,)),
            dma((3, nvar)),
            dma((3, nvar)),
            dma((cell_count,)),
            dma((cell_count,)),
        ],
        compiler_params=pltpu.CompilerParams(
            collective_id=0, has_side_effects=True, vmem_limit_bytes=32 * 1024 * 1024
        ),
    )(jnp.transpose(snapshots, (1, 0, 2)), volumes.reshape(1, cells), freq_index, block_start)
    return jnp.transpose(modes, (2, 0, 1, 3)), triangle


def solution(mesh):
    placed = (P("tm", None, "cell"), P("cell"), P(), P())
    return jax.shard_map(
        on_device,
        mesh=mesh,
        in_specs=placed,
        out_specs=(P("tm", None, None, "cell"), P("tm", None, None)),
        check_vma=False,
    )
```

time: 87 us -> 26.5 us (0.30)
  waiting for transfers between devices: 29.2 us -> 0 us
  Pallas kernels: 0 us -> 21 us
  other arithmetic: 18.1 us -> 0 us
  starting transfers between devices: 15.4 us -> 0 us
  local copies, waits for them, and re-layouts: 18.6 us -> 4.7 us
  matrix products: 4.37 us -> 0 us
    all_to_all x2 -> x0, waiting for transfers between devices: 24.5 us -> none  [the longest x1 18.3 us: on_device(): lax.all_to_all(snapshots, 'tm', split_axis=2, concat_axis=0, tiled=True)]
    pallas_call x0 -> x1, Pallas kernels: none -> 21 us  [on_device(): pl.pallas_call(functools.partial(kernel, sizes), out_shape=(jax.ShapeDtyp...]
    another operation x16 -> x0, other arithmetic: 9.51 us -> none  [the longest x10 5.95 us: on_device(): lower = jnp.linalg.cholesky(outer_sum(lower, partner))]
    all_to_all x2 -> x0, starting transfers between devices: 7.97 us -> none  [the longest x1 4.34 us: on_device(): lax.all_to_all(snapshots, 'tm', split_axis=2, concat_axis=0, tiled=True)]
    unnamed x13 -> x8, local copies, waits for them, and re-layouts: 11.9 us -> 4 us
    all_to_all x2 -> x0, other arithmetic: 7.55 us -> none  [the longest x1 6.05 us: on_device(): lax.all_to_all(snapshots, 'tm', split_axis=2, concat_axis=0, tiled=True)]
    ppermute x3 -> x0, starting transfers between devices: 7.44 us -> none  [partner_2(): return lax.ppermute(block, axis, route)]
    ppermute x3 -> x0, waiting for transfers between devices: 4.74 us -> none  [partner_2(): return lax.ppermute(block, axis, route)]
  transfers between devices with their start and end apart: 5 -> 0, of which waited for: 5 -> 0; matrix products, arithmetic and copies ran while one was open for 1% -> 0% of each run, Pallas kernels for 0% -> 0%
where the time goes in v1:
time: 26.5 us; the launch traced here: 26.3 us
  Pallas kernels  21 us (79%)
  local copies, waits for them, and re-layouts  4.7 us (18%)
  between operations  0.64 us (2%)
    pallas_call x1, Pallas kernels, on_device(): pl.pallas_call(functools.partial(kernel, sizes), out_shape=(jax.ShapeDtyp...  21 us
    unnamed x8, local copies, waits for them, and re-layouts  4 us
    reshape x1, local copies, waits for them, and re-layouts, on_device(): volumes.reshape(1, cells)  0.69 us

profile of v1, /device:TPU:0, one launch (start us, length us, event | category | flops | bytes accessed | tf_op | source)
XLA Modules:
  0.0 26.3 jit_solution(3374720753235361740)
XLA Ops:
  0.6 0.7 %reshape.7.vol_ref = f32[1,768]{1,0:T(1,128)S(1)} reshape(f32[768]{0:T(1024)} %param.5) | data formatting | bytes 6144 | tf_op jit(solution)/shard_map/reshape | solution.py:308
  1.3 0.0 copy-start
  1.3 1.4 %copy-done = f32[96,5,768]{2,0,1:T(8,128)S(1)} copy-done((f32[96,5,768]{2,0,1:T(8,128)S(1)}, f32[96,5,768]{2,0,1:T(8,128)}, u32[]{:S(2)}) %copy-start) | copy-done | bytes 1474584
  2.7 0.0 copy-start.1
  2.7 0.7 %copy-done.1 = s32[8]{0:T(128)S(1)} copy-done((s32[8]{0:T(128)S(1)}, s32[8]{0:T(128)}, u32[]{:S(2)}) %copy-start.1) | copy-done | bytes 56
  3.3 0.0 copy-start.2
  3.4 0.7 %copy-done.2 = s32[5]{0:T(128)S(1)} copy-done((s32[5]{0:T(128)S(1)}, s32[5]{0:T(128)}, u32[]{:S(2)}) %copy-start.2) | copy-done | bytes 44
  4.0 21.0 %shard_map.59 = (f32[10,5,2,768]{3,2,1,0:T(2,128)S(1)}, f32[2,10,10]{2,1,0:T(8,128)S(1)}) custom-call(f32[5,96,768]{2,1,0:T(8,128)S(1)} %bitcast.2, f32[1,768]{1,0:T(1,128)S(1)} %reshape.7.vol_ref, s32[8]{0:T(128)S(1)} %copy-done.1, s32[5]{0:T(128)S(1)} %copy-done.2), custom_call_target="tpu_custom_call" | custom-call | tf_op jit(solution)/shard_map/pallas_call | solution.py:275
  25.0 0.6 %copy.6 = f32[2,10,10]{2,0,1:T(2,128)} copy(f32[2,10,10]{2,1,0:T(8,128)S(1)} %get-tuple-element.7) | data formatting | bytes 1600
  25.6 0.7 %copy.8 = f32[2,10,5,768]{3,0,2,1:T(2,128)} copy(f32[2,10,5,768]{3,0,2,1:T(2,128)S(1)} %bitcast.3) | data formatting | bytes 614400
Async XLA Ops:
  1.3 1.4 %copy-start = (f32[96,5,768]{2,0,1:T(8,128)S(1)}, f32[96,5,768]{2,0,1:T(8,128)}, u32[]{:S(2)}) copy-start(f32[96,5,768]{2,0,1:T(8,128)} %param.4) | copy-start | bytes 4423684
  2.7 0.7 %copy-start.1 = (s32[8]{0:T(128)S(1)}, s32[8]{0:T(128)}, u32[]{:S(2)}) copy-start(s32[8]{0:T(128)} %freq_ref.1) | copy-start | bytes 100
  3.3 0.7 %copy-start.2 = (s32[5]{0:T(128)S(1)}, s32[5]{0:T(128)}, u32[]{:S(2)}) copy-start(s32[5]{0:T(128)} %start_ref.1) | copy-start | bytes 64

commit v2 on v1

--- a/solution.py
+++ b/solution.py
@@ -1,4 +1,5 @@
 import functools
+import math
 
 import jax
 import jax.numpy as jnp
@@ -29,19 +30,36 @@
     )
 
 
-def kernel(
+def half_sine_squared(step):
+    near = ((step + NFFT // 2) & (NFFT - 1)) - NFFT // 2
+    u = near.astype(F32) * (math.pi / NFFT)
+    square = u * u
+    total = jnp.full_like(u, 1.0 / math.factorial(13))
+    for power in (11, 9, 7, 5, 3, 1):
+        sign = 1.0 if power % 4 == 1 else -1.0
+        total = total * square + sign / math.factorial(power)
+    sine = u * total
+    return sine * sine
+
+
+def gather_kernel(
     sizes,
     x_ref,
+    vol_hbm,
+    freq_hbm,
+    start_hbm,
+    wcat_hbm,
+    total_hbm,
+    wcat,
+    total_ref,
+    snap,
+    part,
+    got,
+    grams,
     vol_ref,
     freq_ref,
     start_ref,
-    modes_ref,
-    tri_ref,
-    snap,
-    part,
-    got,
-    wcat,
-    grams,
+    small_sem,
     local_sem,
     xsend_sem,
     xrecv_sem,
@@ -49,6 +67,7 @@
     precv_sem,
     gsend_sem,
     grecv_sem,
+    out_sem,
 ):
     cell_count, tdev, nvar, cells, nf, nb = sizes
     fdev = nf // 4
@@ -67,6 +86,13 @@
     my_cells = pl.ds(pl.multiple_of(core * half, 128), half)
     other_cells = pl.ds(pl.multiple_of((1 - core) * half, 128), half)
 
+    small = []
+    for k, (src, dst) in enumerate(
+        ((freq_hbm, freq_ref), (start_hbm, start_ref), (vol_hbm, vol_ref))
+    ):
+        copy = pltpu.make_async_copy(src, dst, small_sem.at[k])
+        copy.start()
+        small.append(copy)
     local = []
     for v in range(nvar):
         copy = pltpu.make_async_copy(
@@ -86,6 +112,23 @@
             device_id_type=MESH,
         )
 
+    pl.semaphore_wait(barrier, len(targets) + cell_count - 1)
+
+    exchange = []
+    for v in range(nvar):
+        copy = pltpu.make_async_remote_copy(
+            src_ref=x_ref.at[v, :, other_cells],
+            dst_ref=snap.at[v, my_rows, :],
+            send_sem=xsend_sem.at[v],
+            recv_sem=xrecv_sem.at[v],
+            device_id={"tm": partner},
+            device_id_type=MESH,
+        )
+        copy.start()
+        exchange.append(copy)
+
+    for copy in small:
+        copy.wait()
     row = lax.broadcasted_iota(jnp.int32, (rows, span), 0)
     time = lax.broadcasted_iota(jnp.int32, (rows, span), 1) + group * span
     imag = row % 2
@@ -99,26 +142,8 @@
         freq = jnp.where(row_freq == f, freq_ref[f], freq)
     tau = time - start
     valid = (tau >= 0) & (tau < NFFT)
-    turn = 2.0 * jnp.pi / NFFT
-    hann = jnp.where(valid, 0.5 - 0.5 * jnp.cos((tau & (NFFT - 1)).astype(F32) * turn), 0.0)
-
-    pl.semaphore_wait(barrier, len(targets) + cell_count - 1)
-
-    exchange = []
-    for v in range(nvar):
-        copy = pltpu.make_async_remote_copy(
-            src_ref=x_ref.at[v, :, other_cells],
-            dst_ref=snap.at[v, my_rows, :],
-            send_sem=xsend_sem.at[v],
-            recv_sem=xrecv_sem.at[v],
-            device_id={"tm": partner},
-            device_id_type=MESH,
-        )
-        copy.start()
-        exchange.append(copy)
-
-    phase = (freq * tau + imag * (NFFT // 4)) & (NFFT - 1)
-    table = hann * jnp.cos(phase.astype(F32) * turn)
+    hann = jnp.where(valid, half_sine_squared(tau), 0.0)
+    table = hann * (1.0 - 2.0 * half_sine_squared(freq * tau + imag * (NFFT // 4)))
     th, tmid, tl = split3(table)
     table3 = jnp.concatenate([th, tmid, tl], axis=0)
 
@@ -130,8 +155,8 @@
         a = jnp.dot(table3, sh, preferred_element_type=F32)
         b = jnp.dot(table3[: 2 * rows], sm, preferred_element_type=F32)
         c = jnp.dot(th, sl, preferred_element_type=F32)
-        small = a[2 * rows :] + b[rows:] + c
-        part[v] = a[:rows] + ((a[rows : 2 * rows] + b[:rows]) + small)
+        least = a[2 * rows :] + b[rows:] + c
+        part[v] = a[:rows] + ((a[rows : 2 * rows] + b[:rows]) + least)
         for k, target in enumerate(targets):
             copy = pltpu.make_async_remote_copy(
                 src_ref=part.at[v, pl.ds(pl.multiple_of(target * per, 8), per), :],
@@ -145,8 +170,9 @@
             sends.append((v, copy))
         got[group, v, :, my_cells] = part[v, pl.ds(pl.multiple_of(tm * per, 8), per), :]
 
-    root = jnp.sqrt(vol_ref[...])
+    root = jnp.sqrt(vol_ref[...].reshape(1, cells))
     gram = jnp.zeros((3 * ROWS, 128), F32)
+    outs = []
     for v in range(nvar):
         for w, copy in sends:
             if w == v:
@@ -156,8 +182,11 @@
         second = pltpu.roll(jnp.concatenate([got[1, v], pad], axis=0), 2 * fdev, 0)
         weighted = (first + second) * root
         wh, wm, wl = split3(weighted)
-        wcat[v] = jnp.concatenate([wh, wm, wl, wh, wm, wh], axis=0)
         lhs = jnp.concatenate([wh, wm, wl], axis=0)
+        wcat[v] = lhs
+        copy = pltpu.make_async_copy(wcat.at[v], wcat_hbm.at[v], out_sem.at[v])
+        copy.start()
+        outs.append(copy)
         rhs = jnp.concatenate([wh, wm, wl, jnp.zeros_like(wh)], axis=0)
         gram = gram + lax.dot_general(lhs, rhs, NT, preferred_element_type=F32)
 
@@ -189,6 +218,47 @@
     for q in range(1, cell_count):
         total = total + grams[q]
 
+    total_ref[...] = total
+    copy = pltpu.make_async_copy(total_ref, total_hbm, out_sem.at[nvar])
+    copy.start()
+    outs.append(copy)
+
+    for copy in exchange:
+        copy.wait_send()
+    for _, copy in sends:
+        copy.wait_send()
+    for copy in gsends:
+        copy.wait_send()
+    for copy in outs:
+        copy.wait()
+
+
+def modes_kernel(
+    sizes,
+    wcat_hbm,
+    total_hbm,
+    modes_hbm,
+    tri_hbm,
+    wcat,
+    total_ref,
+    modes_ref,
+    tri_ref,
+    in_sem,
+    out_sem,
+):
+    cell_count, tdev, nvar, cells, nf, nb = sizes
+    fdev = nf // 4
+    total_in = pltpu.make_async_copy(total_hbm, total_ref, in_sem.at[nvar])
+    total_in.start()
+    wcat_in = []
+    for v in range(nvar):
+        copy = pltpu.make_async_copy(wcat_hbm.at[v], wcat.at[v], in_sem.at[v])
+        copy.start()
+        wcat_in.append(copy)
+    total_in.wait()
+    lane = lax.broadcasted_iota(jnp.int32, (ROWS, 128), 1)
+    line = lax.broadcasted_iota(jnp.int32, (ROWS, 128), 0)
+    total = total_ref[...]
     pieces = [total] + [pltpu.roll(total, 128 - ROWS * q, 1) for q in range(1, ROWS // 8)]
     full = jnp.concatenate(pieces, axis=0)
     aug = jnp.where(lane < ROWS, full, jnp.where(lane - ROWS == line, 1.0, 0.0))
@@ -217,7 +287,8 @@
     in_row = lax.broadcasted_iota(jnp.int32, (ROWS, ROWS), 1)
     place = ((in_row % 2) * nb + in_row // (2 * fdev)) * fdev + (in_row // 2) % fdev
     permute = jnp.where((in_row < used) & (out_row == place), 1.0, 0.0)
-    solve = exact_dot(permute, aug) * jnp.sqrt(F32(total_rows))
+    ordered = exact_dot(permute, aug)
+    solve = ordered * jnp.sqrt(F32(total_rows))
     solve = jnp.where((lane >= ROWS) & (lane < 2 * ROWS), solve, 0.0)
     solve = solve + pltpu.roll(solve, 2 * ROWS, 1)
     solve = solve + pltpu.roll(solve, ROWS, 1)
@@ -229,36 +300,38 @@
         ],
         axis=1,
     )[:, : 6 * ROWS].astype(BF16)
-    for v in range(nvar):
-        modes = jnp.dot(lhs, wcat[v], preferred_element_type=F32)
+    copies = []
+    for v in range(nvar):
+        wcat_in[v].wait()
+        held = wcat[v]
+        rhs = jnp.concatenate([held, held[: 2 * ROWS], held[:ROWS]], axis=0)
+        modes = jnp.dot(lhs, rhs, preferred_element_type=F32)
         for j in range(columns):
-            modes_ref[j, v, :, :] = modes[j * fdev : (j + 1) * fdev, :]
-
-    tri_row = lax.broadcasted_iota(jnp.int32, (16, ROWS), 0)
-    tri_in = lax.broadcasted_iota(jnp.int32, (16, ROWS), 1)
+            modes_ref[v, j, :, :] = modes[j * fdev : (j + 1) * fdev, :]
+        copy = pltpu.make_async_copy(modes_ref.at[v], modes_hbm.at[:, v], out_sem.at[v])
+        copy.start()
+        copies.append(copy)
+
+    tri_scale = F32(1.0) / jnp.sqrt(F32(total_rows * NFFT))
     tri_out = lax.broadcasted_iota(jnp.int32, (16, 128), 0)
-    tri_lane = lax.broadcasted_iota(jnp.int32, (16, 128), 1)
-
-    def picks(out, inner, f):
-        match = ((inner % 2) * nb + inner // (2 * fdev) == out) & ((inner // 2) % fdev == f)
-        return jnp.where(match & (inner < used), 1.0, 0.0)
-
-    tri_scale = F32(1.0) / jnp.sqrt(F32(total_rows * NFFT))
-    upper = lax.broadcasted_iota(jnp.int32, (16, 16), 0) <= lax.broadcasted_iota(
-        jnp.int32, (16, 16), 1
-    )
+    tri_in = lax.broadcasted_iota(jnp.int32, (16, 128), 1)
+    tri_row = lax.broadcasted_iota(jnp.int32, (ROWS, 16), 0)
+    tri_lane = lax.broadcasted_iota(jnp.int32, (ROWS, 16), 1)
+    tri = jnp.zeros((ROWS, 16), F32)
     for f in range(fdev):
-        left = exact_dot(picks(tri_row, tri_in, f), aug)
-        both = exact_dot(left, picks(tri_out, tri_lane, f), NT)
-        tri = jnp.where(upper, both * tri_scale, 0.0)
-        tri_ref[f] = tri[:columns, :columns]
-
-    for copy in exchange:
-        copy.wait_send()
-    for _, copy in sends:
-        copy.wait_send()
-    for copy in gsends:
-        copy.wait_send()
+        match = ((tri_in % 2) * nb + tri_in // (2 * fdev) == tri_out) & (
+            (tri_in // 2) % fdev == f
+        )
+        picks = jnp.where(match & (tri_in < used), 1.0, 0.0)
+        tri = jnp.where(tri_row % fdev == f, exact_dot(ordered, picks, NT), tri)
+    tri = jnp.where(tri_row // fdev <= tri_lane, tri * tri_scale, 0.0)
+    for j in range(columns):
+        tri_ref[j] = tri[j * fdev : (j + 1) * fdev, :columns]
+    copy = pltpu.make_async_copy(tri_ref, tri_hbm, out_sem.at[nvar])
+    copy.start()
+    copies.append(copy)
+    for copy in copies:
+        copy.wait()
 
 
 def on_device(snapshots, volumes, freq_index, block_start):
@@ -272,28 +345,26 @@
     per = kept * 2 * fdev
     sizes = (cell_count, tdev, nvar, cells, nf, nb)
     dma = pltpu.SemaphoreType.DMA
-    modes, triangle = pl.pallas_call(
-        functools.partial(kernel, sizes),
+    hbm = pl.BlockSpec(memory_space=pltpu.HBM)
+    wcat, total = pl.pallas_call(
+        functools.partial(gather_kernel, sizes),
         out_shape=(
-            jax.ShapeDtypeStruct((columns, nvar, fdev, cells), F32),
-            jax.ShapeDtypeStruct((fdev, columns, columns), F32),
+            jax.ShapeDtypeStruct((nvar, 3 * ROWS, cells), BF16),
+            jax.ShapeDtypeStruct((8, 128), F32),
         ),
-        in_specs=[
-            pl.BlockSpec(memory_space=pl.ANY),
-            pl.BlockSpec(memory_space=pltpu.VMEM),
-            pl.BlockSpec(memory_space=pltpu.SMEM),
-            pl.BlockSpec(memory_space=pltpu.SMEM),
-        ],
-        out_specs=(
-            pl.BlockSpec(memory_space=pltpu.VMEM),
-            pl.BlockSpec(memory_space=pltpu.VMEM),
-        ),
+        in_specs=[hbm] * 4,
+        out_specs=(hbm, hbm),
         scratch_shapes=[
+            pltpu.VMEM((nvar, 3 * ROWS, cells), BF16),
+            pltpu.VMEM((8, 128), F32),
             pltpu.VMEM((nvar, 2 * tdev, half), F32),
             pltpu.VMEM((nvar, nf * 2 * kept, half), F32),
             pltpu.VMEM((2, nvar, per, cells), F32),
-            pltpu.VMEM((nvar, 6 * ROWS, cells), BF16),
             pltpu.VMEM((cell_count, 8, 128), F32),
+            pltpu.VMEM((cells,), F32),
+            pltpu.SMEM((nf,), jnp.int32),
+            pltpu.SMEM((nb,), jnp.int32),
+            dma((3,)),
             dma((nvar,)),
             dma((nvar,)),
             dma((nvar,)),
@@ -301,12 +372,31 @@
             dma((3, nvar)),
             dma((cell_count,)),
             dma((cell_count,)),
+            dma((nvar + 1,)),
         ],
         compiler_params=pltpu.CompilerParams(
-            collective_id=0, has_side_effects=True, vmem_limit_bytes=32 * 1024 * 1024
+            collective_id=0, has_side_effects=True, vmem_limit_bytes=63 * 1024 * 1024
         ),
-    )(jnp.transpose(snapshots, (1, 0, 2)), volumes.reshape(1, cells), freq_index, block_start)
-    return jnp.transpose(modes, (2, 0, 1, 3)), triangle
+    )(jnp.transpose(snapshots, (1, 0, 2)), volumes, freq_index, block_start)
+    modes, triangle = pl.pallas_call(
+        functools.partial(modes_kernel, sizes),
+        out_shape=(
+            jax.ShapeDtypeStruct((columns, nvar, fdev, cells), F32),
+            jax.ShapeDtypeStruct((columns, fdev, columns), F32),
+        ),
+        in_specs=[hbm, hbm],
+        out_specs=(hbm, hbm),
+        scratch_shapes=[
+            pltpu.VMEM((nvar, 3 * ROWS, cells), BF16),
+            pltpu.VMEM((8, 128), F32),
+            pltpu.VMEM((nvar, columns, fdev, cells), F32),
+            pltpu.VMEM((columns, fdev, columns), F32),
+            dma((nvar + 1,)),
+            dma((nvar + 1,)),
+        ],
+        compiler_params=pltpu.CompilerParams(vmem_limit_bytes=63 * 1024 * 1024),
+    )(wcat, total)
+    return jnp.transpose(modes, (2, 0, 1, 3)), jnp.transpose(triangle, (1, 0, 2))
 
 
 def solution(mesh):

time: 26.5 us -> 23.7 us (0.89)
  local copies, waits for them, and re-layouts: 4.7 us -> 0 us
  Pallas kernels: 21 us -> 22.8 us
    unnamed x8 -> x0, local copies, waits for them, and re-layouts: 4 us -> none
    pallas_call x1 -> x2, Pallas kernels: 21 us -> 22.8 us  [the longest x1 19.2 us: on_device(): pl.pallas_call(functools.partial(gather_kernel, sizes), out_shape=(jax.Sh...]
    reshape x1 -> x0, local copies, waits for them, and re-layouts: 0.69 us -> none  [on_device(): volumes.reshape(1, cells)]
where the time goes in v2:
time: 23.7 us; the launch traced here: 23.5 us
  Pallas kernels  22.8 us (96%)
  between operations  0.64 us (3%)
    pallas_call x1, Pallas kernels, on_device(): pl.pallas_call(functools.partial(gather_kernel, sizes), out_shape=(jax.Sh...  19.2 us
    pallas_call x1, Pallas kernels, on_device(): pl.pallas_call(functools.partial(modes_kernel, sizes), out_shape=(jax.Sha...  3.6 us

profile of v2, /device:TPU:0, one launch (start us, length us, event | category | flops | bytes accessed | tf_op | source)
XLA Modules:
  0.0 23.5 jit_solution(7906428318595511658)
XLA Ops:
  0.6 19.2 %shard_map.59 = (bf16[5,96,768]{2,1,0:T(8,128)(2,1)}, f32[8,128]{1,0:T(8,128)}) custom-call(f32[5,96,768]{2,1,0:T(8,128)} %bitcast.3, f32[768]{0:T(1024)} %vol_hbm.1, s32[8]{0:T(128)} %freq_hbm.1, s32[5]{0:T(128)} %start_hbm.1), custom_call_target="tpu_custom_call" | custom-call | tf_op jit(solution)/shard_map/pallas_call | solution.py:349
  19.9 3.6 %shard_map.60 = (f32[10,5,2,768]{3,2,1,0:T(2,128)}, f32[10,2,10]{2,1,0:T(2,128)}) custom-call(bf16[5,96,768]{2,1,0:T(8,128)(2,1)} %get-tuple-element.6.wcat_hbm, f32[8,128]{1,0:T(8,128)} %get-tuple-element.7.total_hbm), custom_call_target="tpu_custom_call" | custom-call | tf_op jit(solution)/shard_map/pallas_call | solution.py:381

commit v3 on v2

v3 whole, which is shorter than its diff:
```python
import functools
import math

import jax
import jax.numpy as jnp
from jax import lax
from jax.experimental import pallas as pl
from jax.experimental.pallas import tpu as pltpu
from jax.sharding import PartitionSpec as P

NFFT = 128
MESH = pl.DeviceIdType.MESH
F32 = jnp.float32
BF16 = jnp.bfloat16
NT = (((1,), (1,)), ((), ()))
ROWS = 32


def split3(a):
    high = a.astype(BF16)
    rest = a - high.astype(F32)
    middle = rest.astype(BF16)
    low = (rest - middle.astype(F32)).astype(BF16)
    return high, middle, low


def half_sine_squared(step):
    near = ((step + NFFT // 2) & (NFFT - 1)) - NFFT // 2
    u = near.astype(F32) * (math.pi / NFFT)
    square = u * u
    total = jnp.full_like(u, 1.0 / math.factorial(13))
    for power in (11, 9, 7, 5, 3, 1):
        sign = 1.0 if power % 4 == 1 else -1.0
        total = total * square + sign / math.factorial(power)
    sine = u * total
    return sine * sine


def gather_kernel(
    sizes,
    x_ref,
    vol_hbm,
    freq_hbm,
    start_hbm,
    wcat_hbm,
    grams_hbm,
    wcat,
    packed_ref,
    snap,
    part,
    got,
    vol_ref,
    freq_ref,
    start_ref,
    small_sem,
    local_sem,
    xsend_sem,
    xrecv_sem,
    psend_sem,
    precv_sem,
    gsend_sem,
    grecv_sem,
    out_sem,
):
    cell_count, tdev, nvar, cells, nf, nb = sizes
    fdev = nf // 4
    kept = nb - 1
    half = cells // 2
    span = 2 * tdev
    per = kept * 2 * fdev
    rows = nf * 2 * kept
    cell = lax.axis_index("cell")
    tm = lax.axis_index("tm")
    group, core = tm // 2, lax.rem(tm, 2)
    partner = group * 2 + 1 - core
    targets = ((1 - group) * 2 + core, (1 - group) * 2 + 1 - core, partner)

    my_rows = pl.ds(pl.multiple_of(core * tdev, 8), tdev)
    my_cells = pl.ds(pl.multiple_of(core * half, 128), half)
    other_cells = pl.ds(pl.multiple_of((1 - core) * half, 128), half)

    barrier = pltpu.get_barrier_semaphore()
    for target in targets:
        pl.semaphore_signal(barrier, inc=1, device_id={"tm": target}, device_id_type=MESH)
    for step in range(1, cell_count):
        pl.semaphore_signal(
            barrier,
            inc=1,
            device_id={"cell": lax.rem(cell + step, cell_count)},
            device_id_type=MESH,
        )

    small = []
    for k, (src, dst) in enumerate(
        ((freq_hbm, freq_ref), (start_hbm, start_ref), (vol_hbm, vol_ref))
    ):
        copy = pltpu.make_async_copy(src, dst, small_sem.at[k])
        copy.start()
        small.append(copy)
    local = []
    for v in range(nvar):
        copy = pltpu.make_async_copy(
            x_ref.at[v, :, my_cells], snap.at[v, my_rows, :], local_sem.at[v]
        )
        copy.start()
        local.append(copy)

    pl.semaphore_wait(barrier, len(targets) + cell_count - 1)

    exchange = []
    for v in range(nvar):
        copy = pltpu.make_async_remote_copy(
            src_ref=x_ref.at[v, :, other_cells],
            dst_ref=snap.at[v, my_rows, :],
            send_sem=xsend_sem.at[v],
            recv_sem=xrecv_sem.at[v],
            device_id={"tm": partner},
            device_id_type=MESH,
        )
        exchange.append(copy)
    for v in range(min(2, nvar)):
        exchange[v].start()

    for copy in small:
        copy.wait()
    row = lax.broadcasted_iota(jnp.int32, (rows, span), 0)
    time = lax.broadcasted_iota(jnp.int32, (rows, span), 1) + group * span
    imag = (row // fdev) % 2
    row_block = (row // (2 * fdev)) % kept
    row_freq = (row // per) * fdev + row % fdev
    start = jnp.zeros((rows, span), jnp.int32)
    for b in range(kept):
        start = jnp.where(row_block == b, start_ref[group + b], start)
    freq = jnp.zeros((rows, span), jnp.int32)
    for f in range(nf):
        freq = jnp.where(row_freq == f, freq_ref[f], freq)
    tau = time - start
    valid = (tau >= 0) & (tau < NFFT)
    hann = jnp.where(valid, half_sine_squared(tau), 0.0)
    table = hann * (1.0 - 2.0 * half_sine_squared(freq * tau + imag * (NFFT // 4)))
    th, tmid, tl = split3(table)
    table3 = jnp.concatenate([th, tmid, tl], axis=0)

    sends = []
    for v in range(nvar):
        local[v].wait()
        exchange[v].wait_recv()
        if v + 2 < nvar:
            exchange[v + 2].start()
        sh, sm, sl = split3(snap[v])
        a = jnp.dot(table3, sh, preferred_element_type=F32)
        b = jnp.dot(table3[: 2 * rows], sm, preferred_element_type=F32)
        c = jnp.dot(th, sl, preferred_element_type=F32)
        least = a[2 * rows :] + b[rows:] + c
        part[v] = a[:rows] + ((a[rows : 2 * rows] + b[:rows]) + least)
        for k, target in enumerate(targets):
            copy = pltpu.make_async_remote_copy(
                src_ref=part.at[v, pl.ds(pl.multiple_of(target * per, 8), per), :],
                dst_ref=got.at[group, v, :, my_cells],
                send_sem=psend_sem.at[k, v],
                recv_sem=precv_sem.at[k, v],
                device_id={"tm": target},
                device_id_type=MESH,
            )
            copy.start()
            sends.append((v, copy))
        got[group, v, :, my_cells] = part[v, pl.ds(pl.multiple_of(tm * per, 8), per), :]

    root = jnp.sqrt(vol_ref[...].reshape(1, cells))
    gram = jnp.zeros((3 * ROWS, 128), F32)
    outs = []
    for v in range(nvar):
        for w, copy in sends:
            if w == v:
                copy.wait_recv()
        pad = jnp.zeros((ROWS - per, cells), F32)
        first = jnp.concatenate([got[0, v], pad], axis=0)
        second = pltpu.roll(jnp.concatenate([got[1, v], pad], axis=0), 2 * fdev, 0)
        weighted = (first + second) * root
        wh, wm, wl = split3(weighted)
        lhs = jnp.concatenate([wh, wm, wl], axis=0)
        wcat[v] = lhs
        copy = pltpu.make_async_copy(wcat.at[v], wcat_hbm.at[v], out_sem.at[v])
        copy.start()
        outs.append(copy)
        rhs = jnp.concatenate([wh, wm, wl, jnp.zeros_like(wh)], axis=0)
        gram = gram + lax.dot_general(lhs, rhs, NT, preferred_element_type=F32)

    gram = gram[:ROWS] + (gram[ROWS : 2 * ROWS] + gram[2 * ROWS :])
    lane = lax.broadcasted_iota(jnp.int32, (8, 128), 1)
    packed = jnp.zeros((8, 128), F32)
    for q in range(ROWS // 8):
        if 8 * q < 2 * nb * fdev:
            group_rows = gram[8 * q : 8 * q + 8]
            folded = sum(
                pltpu.roll(group_rows, ROWS * (q - s) % 128, 1) if q != s else group_rows
                for s in range(3)
            )
            packed = jnp.where(lane // ROWS == q, folded, packed)
    packed_ref[...] = packed

    own = pltpu.make_async_copy(packed_ref, grams_hbm.at[cell], out_sem.at[nvar])
    own.start()
    outs.append(own)
    gsends = []
    for step in range(1, cell_count):
        copy = pltpu.make_async_remote_copy(
            src_ref=packed_ref,
            dst_ref=grams_hbm.at[cell],
            send_sem=gsend_sem.at[step],
            recv_sem=grecv_sem.at[step],
            device_id={"cell": lax.rem(cell + step, cell_count)},
            device_id_type=MESH,
        )
        copy.start()
        gsends.append(copy)
    for copy in exchange:
        copy.wait_send()
    for _, copy in sends:
        copy.wait_send()
    for copy in outs:
        copy.wait()
    for copy in gsends:
        copy.wait_send()
        copy.wait_recv()


def modes_kernel(
    sizes,
    wcat_hbm,
    grams_hbm,
    modes_hbm,
    tri_hbm,
    wcat,
    grams,
    modes_ref,
    tri_ref,
    in_sem,
    out_sem,
):
    cell_count, tdev, nvar, cells, nf, nb = sizes
    fdev = nf // 4
    columns = 2 * nb
    used = fdev * columns
    height = -(-used // 8) * 8
    grams_in = pltpu.make_async_copy(grams_hbm, grams, in_sem.at[nvar])
    grams_in.start()
    wcat_in = []
    for v in range(nvar):
        copy = pltpu.make_async_copy(wcat_hbm.at[v], wcat.at[v], in_sem.at[v])
        copy.start()
        wcat_in.append(copy)

    lane = lax.broadcasted_iota(jnp.int32, (height, 128), 1)
    line = lax.broadcasted_iota(jnp.int32, (height, 128), 0)
    order = ((line // fdev) % 2) * nb + line // (2 * fdev)
    order = jnp.where(line < used, order, -1)
    bases = [(j % nb) * 2 * fdev + (j // nb) * fdev for j in range(columns)]
    tile_lane = lax.broadcasted_iota(jnp.int32, (8, 128), 1)
    tile_freq = lax.broadcasted_iota(jnp.int32, (8, 128), 0) % fdev

    grams_in.wait()
    total = grams[0]
    for q in range(1, cell_count):
        total = total + grams[q]

    def spread(base):
        pieces = []
        for q in range(height // 8):
            hit = tile_lane == ROWS * q + base + tile_freq
            piece = jnp.sum(jnp.where(hit, total, 0.0), axis=1, keepdims=True)
            pieces.append(jnp.broadcast_to(piece, (8, 128)))
        return jnp.concatenate(pieces, axis=0)

    def pivot_rows(a, base):
        pivot = jnp.broadcast_to(a[base : base + 1, :], (height, 128))
        for f in range(1, fdev):
            pivot = jnp.where(line % fdev == f, a[base + f : base + f + 1, :], pivot)
        return pivot

    gram = [spread(base) for base in bases]
    inverse = jnp.where(lane % ROWS == line, 1.0, 0.0)
    diagonal = jnp.ones((height, 128), F32)
    upper = jnp.zeros((height, 128), F32)
    for j in range(columns):
        diagonal = jnp.where(order == j, gram[j], diagonal)
        upper = jnp.where((lane == j) & (order <= j), gram[j], upper)
        if j + 1 < columns:
            factor = jnp.where(order > j, gram[j] / pivot_rows(gram[j], bases[j]), 0.0)
            for k in range(j + 1, columns):
                gram[k] = gram[k] - factor * pivot_rows(gram[k], bases[j])
            inverse = inverse - factor * pivot_rows(inverse, bases[j])
    scale = 1.0 / jnp.sqrt(diagonal)

    total_rows = nvar * cells * cell_count
    solve = inverse * (scale * jnp.sqrt(F32(total_rows)))
    solve = jnp.concatenate([solve, jnp.zeros((ROWS - height, 128), F32)], axis=0)
    eh, em, el = [e.astype(F32) for e in split3(solve)]
    wide = lax.broadcasted_iota(jnp.int32, (ROWS, 128), 1)
    lhs = jnp.concatenate(
        [jnp.where(wide < 3 * ROWS, eh, em), jnp.where(wide < ROWS, em, el)], axis=1
    )[:, : 6 * ROWS].astype(BF16)
    copies = []
    for v in range(nvar):
        wcat_in[v].wait()
        held = wcat[v]
        rhs = jnp.concatenate([held, held[: 2 * ROWS], held[:ROWS]], axis=0)
        modes = jnp.dot(lhs, rhs, preferred_element_type=F32)
        for j, base in enumerate(bases):
            modes_ref[v, j, :, :] = modes[base : base + fdev, :]
        copy = pltpu.make_async_copy(modes_ref.at[v], modes_hbm.at[:, v], out_sem.at[v])
        copy.start()
        copies.append(copy)
        if v == 0:
            tri = upper * (scale * (F32(1.0) / jnp.sqrt(F32(total_rows * NFFT))))
            for j, base in enumerate(bases):
                tri_ref[j] = tri[base : base + fdev, :columns]
            copy = pltpu.make_async_copy(tri_ref, tri_hbm, out_sem.at[nvar])
            copy.start()
            copies.append(copy)
    for copy in copies:
        copy.wait()


def on_device(snapshots, volumes, freq_index, block_start):
    tdev, nvar, cells = snapshots.shape
    cell_count = lax.axis_size("cell")
    nf, nb = freq_index.shape[0], block_start.shape[0]
    fdev = nf // lax.axis_size("tm")
    columns = 2 * nb
    kept = nb - 1
    half = cells // 2
    per = kept * 2 * fdev
    sizes = (cell_count, tdev, nvar, cells, nf, nb)
    dma = pltpu.SemaphoreType.DMA
    hbm = pl.BlockSpec(memory_space=pltpu.HBM)
    wcat, grams = pl.pallas_call(
        functools.partial(gather_kernel, sizes),
        out_shape=(
            jax.ShapeDtypeStruct((nvar, 3 * ROWS, cells), BF16),
            jax.ShapeDtypeStruct((cell_count, 8, 128), F32),
        ),
        in_specs=[hbm] * 4,
        out_specs=(hbm, hbm),
        scratch_shapes=[
            pltpu.VMEM((nvar, 3 * ROWS, cells), BF16),
            pltpu.VMEM((8, 128), F32),
            pltpu.VMEM((nvar, 2 * tdev, half), F32),
            pltpu.VMEM((nvar, nf * 2 * kept, half), F32),
            pltpu.VMEM((2, nvar, per, cells), F32),
            pltpu.VMEM((cells,), F32),
            pltpu.SMEM((nf,), jnp.int32),
            pltpu.SMEM((nb,), jnp.int32),
            dma((3,)),
            dma((nvar,)),
            dma((nvar,)),
            dma((nvar,)),
            dma((3, nvar)),
            dma((3, nvar)),
            dma((cell_count,)),
            dma((cell_count,)),
            dma((nvar + 1,)),
        ],
        compiler_params=pltpu.CompilerParams(
            collective_id=0, has_side_effects=True, vmem_limit_bytes=63 * 1024 * 1024
        ),
    )(jnp.transpose(snapshots, (1, 0, 2)), volumes, freq_index, block_start)
    modes, triangle = pl.pallas_call(
        functools.partial(modes_kernel, sizes),
        out_shape=(
            jax.ShapeDtypeStruct((columns, nvar, fdev, cells), F32),
            jax.ShapeDtypeStruct((columns, fdev, columns), F32),
        ),
        in_specs=[hbm, hbm],
        out_specs=(hbm, hbm),
        scratch_shapes=[
            pltpu.VMEM((nvar, 3 * ROWS, cells), BF16),
            pltpu.VMEM((cell_count, 8, 128), F32),
            pltpu.VMEM((nvar, columns, fdev, cells), F32),
            pltpu.VMEM((columns, fdev, columns), F32),
            dma((nvar + 1,)),
            dma((nvar + 1,)),
        ],
        compiler_params=pltpu.CompilerParams(vmem_limit_bytes=63 * 1024 * 1024),
    )(wcat, grams)
    return jnp.transpose(modes, (2, 0, 1, 3)), jnp.transpose(triangle, (1, 0, 2))


def solution(mesh):
    placed = (P("tm", None, "cell"), P("cell"), P(), P())
    return jax.shard_map(
        on_device,
        mesh=mesh,
        in_specs=placed,
        out_specs=(P("tm", None, None, "cell"), P("tm", None, None)),
        check_vma=False,
    )
```

time: 23.7 us -> 22.1 us (0.932)
  Pallas kernels: 22.8 us -> 21.3 us
    pallas_call x1, Pallas kernels: 3.6 us -> 2.64 us  [on_device(): pl.pallas_call(functools.partial(modes_kernel, sizes), out_shape=(jax.Sha...]
    pallas_call x1, Pallas kernels: 19.2 us -> 18.7 us  [on_device(): pl.pallas_call(functools.partial(gather_kernel, sizes), out_shape=(jax.Sh...]
where the time goes in v3:
time: 22.1 us; the launch traced here: 22 us
  Pallas kernels  21.3 us (96%)
  between operations  0.64 us (3%)
    pallas_call x1, Pallas kernels, on_device(): pl.pallas_call(functools.partial(gather_kernel, sizes), out_shape=(jax.Sh...  18.7 us
    pallas_call x1, Pallas kernels, on_device(): pl.pallas_call(functools.partial(modes_kernel, sizes), out_shape=(jax.Sha...  2.64 us

profile of v3, /device:TPU:0, one launch (start us, length us, event | category | flops | bytes accessed | tf_op | source)
XLA Modules:
  0.0 22.0 jit_solution(3853770866333640386)
XLA Ops:
  0.6 18.7 %shard_map.59 = (bf16[5,96,768]{2,1,0:T(8,128)(2,1)}, f32[8,8,128]{2,1,0:T(8,128)}) custom-call(f32[5,96,768]{2,1,0:T(8,128)} %bitcast.3, f32[768]{0:T(1024)} %vol_hbm.1, s32[8]{0:T(128)} %freq_hbm.1, s32[5]{0:T(128)} %start_hbm.1), custom_call_target="tpu_custom_call" | custom-call | tf_op jit(solution)/shard_map/pallas_call | solution.py:337
  19.3 2.6 %shard_map.60 = (f32[10,5,2,768]{3,2,1,0:T(2,128)}, f32[10,2,10]{2,1,0:T(2,128)}) custom-call(bf16[5,96,768]{2,1,0:T(8,128)(2,1)} %get-tuple-element.6.wcat_hbm, f32[8,8,128]{2,1,0:T(8,128)} %get-tuple-element.7.grams_hbm), custom_call_target="tpu_custom_call" | custom-call | tf_op jit(solution)/shard_map/pallas_call | solution.py:368

commit v4 on v3

--- a/solution.py
+++ b/solution.py
@@ -22,6 +22,11 @@
     middle = rest.astype(BF16)
     low = (rest - middle.astype(F32)).astype(BF16)
     return high, middle, low
+
+
+def split2(a):
+    high = a.astype(BF16)
+    return high, (a - high.astype(F32)).astype(BF16)
 
 
 def half_sine_squared(step):
@@ -48,6 +53,8 @@
     packed_ref,
     snap,
     part,
+    near,
+    chip,
     got,
     vol_ref,
     freq_ref,
@@ -65,22 +72,16 @@
     cell_count, tdev, nvar, cells, nf, nb = sizes
     fdev = nf // 4
     kept = nb - 1
-    half = cells // 2
-    span = 2 * tdev
     per = kept * 2 * fdev
     rows = nf * 2 * kept
     cell = lax.axis_index("cell")
     tm = lax.axis_index("tm")
     group, core = tm // 2, lax.rem(tm, 2)
     partner = group * 2 + 1 - core
-    targets = ((1 - group) * 2 + core, (1 - group) * 2 + 1 - core, partner)
-
-    my_rows = pl.ds(pl.multiple_of(core * tdev, 8), tdev)
-    my_cells = pl.ds(pl.multiple_of(core * half, 128), half)
-    other_cells = pl.ds(pl.multiple_of((1 - core) * half, 128), half)
+    across = (1 - group) * 2 + core
 
     barrier = pltpu.get_barrier_semaphore()
-    for target in targets:
+    for target in (partner, across):
         pl.semaphore_signal(barrier, inc=1, device_id={"tm": target}, device_id_type=MESH)
     for step in range(1, cell_count):
         pl.semaphore_signal(
@@ -99,80 +100,83 @@
         small.append(copy)
     local = []
     for v in range(nvar):
-        copy = pltpu.make_async_copy(
-            x_ref.at[v, :, my_cells], snap.at[v, my_rows, :], local_sem.at[v]
-        )
+        copy = pltpu.make_async_copy(x_ref.at[v], snap.at[v], local_sem.at[v])
         copy.start()
         local.append(copy)
-
-    pl.semaphore_wait(barrier, len(targets) + cell_count - 1)
-
-    exchange = []
-    for v in range(nvar):
-        copy = pltpu.make_async_remote_copy(
-            src_ref=x_ref.at[v, :, other_cells],
-            dst_ref=snap.at[v, my_rows, :],
-            send_sem=xsend_sem.at[v],
-            recv_sem=xrecv_sem.at[v],
-            device_id={"tm": partner},
-            device_id_type=MESH,
-        )
-        exchange.append(copy)
-    for v in range(min(2, nvar)):
-        exchange[v].start()
 
     for copy in small:
         copy.wait()
-    row = lax.broadcasted_iota(jnp.int32, (rows, span), 0)
-    time = lax.broadcasted_iota(jnp.int32, (rows, span), 1) + group * span
+    row = lax.broadcasted_iota(jnp.int32, (rows, 2 * tdev), 0)
+    time = lax.broadcasted_iota(jnp.int32, (rows, 2 * tdev), 1)
+    time = jnp.where(time < tdev, time, time - tdev) + tm * tdev
     imag = (row // fdev) % 2
     row_block = (row // (2 * fdev)) % kept
-    row_freq = (row // per) * fdev + row % fdev
-    start = jnp.zeros((rows, span), jnp.int32)
+    owner = ((row // per) % 2) * 2 + row // (2 * per)
+    row_freq = owner * fdev + row % fdev
+    start = jnp.zeros_like(row)
     for b in range(kept):
         start = jnp.where(row_block == b, start_ref[group + b], start)
-    freq = jnp.zeros((rows, span), jnp.int32)
+    freq = jnp.zeros_like(row)
     for f in range(nf):
         freq = jnp.where(row_freq == f, freq_ref[f], freq)
     tau = time - start
     valid = (tau >= 0) & (tau < NFFT)
     hann = jnp.where(valid, half_sine_squared(tau), 0.0)
     table = hann * (1.0 - 2.0 * half_sine_squared(freq * tau + imag * (NFFT // 4)))
-    th, tmid, tl = split3(table)
-    table3 = jnp.concatenate([th, tmid, tl], axis=0)
-
-    sends = []
-    for v in range(nvar):
+    th, tl = split2(table)
+    table2 = jnp.concatenate([th, tl], axis=0)
+
+    pair, sends = [], []
+
+    def partial(v):
         local[v].wait()
-        exchange[v].wait_recv()
-        if v + 2 < nvar:
-            exchange[v + 2].start()
-        sh, sm, sl = split3(snap[v])
-        a = jnp.dot(table3, sh, preferred_element_type=F32)
-        b = jnp.dot(table3[: 2 * rows], sm, preferred_element_type=F32)
-        c = jnp.dot(th, sl, preferred_element_type=F32)
-        least = a[2 * rows :] + b[rows:] + c
-        part[v] = a[:rows] + ((a[rows : 2 * rows] + b[:rows]) + least)
-        for k, target in enumerate(targets):
-            copy = pltpu.make_async_remote_copy(
-                src_ref=part.at[v, pl.ds(pl.multiple_of(target * per, 8), per), :],
-                dst_ref=got.at[group, v, :, my_cells],
-                send_sem=psend_sem.at[k, v],
-                recv_sem=precv_sem.at[k, v],
-                device_id={"tm": target},
-                device_id_type=MESH,
-            )
-            copy.start()
-            sends.append((v, copy))
-        got[group, v, :, my_cells] = part[v, pl.ds(pl.multiple_of(tm * per, 8), per), :]
+        sh, sl = split2(snap[v])
+        both = jnp.dot(
+            table2, jnp.concatenate([sh, sl], axis=0), preferred_element_type=F32
+        )
+        part[v] = both[:rows] + both[rows:]
+        if v == 0:
+            pl.semaphore_wait(barrier, 2 + cell_count - 1)
+        theirs = pl.ds(pl.multiple_of((1 - core) * 2 * per, 8), 2 * per)
+        copy = pltpu.make_async_remote_copy(
+            src_ref=part.at[v, theirs, :],
+            dst_ref=near.at[v],
+            send_sem=xsend_sem.at[v],
+            recv_sem=xrecv_sem.at[v],
+            device_id={"tm": partner},
+            device_id_type=MESH,
+        )
+        copy.start()
+        pair.append(copy)
+
+    def forward(v):
+        pair[v].wait_recv()
+        mine = pl.ds(pl.multiple_of(core * 2 * per, 8), 2 * per)
+        chip[v] = part[v, mine, :] + near[v]
+        copy = pltpu.make_async_remote_copy(
+            src_ref=chip.at[v, pl.ds(pl.multiple_of((1 - group) * per, 8), per), :],
+            dst_ref=got.at[group, v],
+            send_sem=psend_sem.at[v],
+            recv_sem=precv_sem.at[v],
+            device_id={"tm": across},
+            device_id_type=MESH,
+        )
+        copy.start()
+        sends.append(copy)
+        got[group, v] = chip[v, pl.ds(pl.multiple_of(group * per, 8), per), :]
+
+    lag = 2
+    for v in range(nvar + lag):
+        if v < nvar:
+            partial(v)
+        if v >= lag:
+            forward(v - lag)
 
     root = jnp.sqrt(vol_ref[...].reshape(1, cells))
     gram = jnp.zeros((3 * ROWS, 128), F32)
     outs = []
     for v in range(nvar):
-        for w, copy in sends:
-            if w == v:
-                copy.wait_recv()
+        sends[v].wait_recv()
         pad = jnp.zeros((ROWS - per, cells), F32)
         first = jnp.concatenate([got[0, v], pad], axis=0)
         second = pltpu.roll(jnp.concatenate([got[1, v], pad], axis=0), 2 * fdev, 0)
@@ -214,9 +218,7 @@
         )
         copy.start()
         gsends.append(copy)
-    for copy in exchange:
-        copy.wait_send()
-    for _, copy in sends:
+    for copy in pair + sends:
         copy.wait_send()
     for copy in outs:
         copy.wait()
@@ -329,7 +331,6 @@
     fdev = nf // lax.axis_size("tm")
     columns = 2 * nb
     kept = nb - 1
-    half = cells // 2
     per = kept * 2 * fdev
     sizes = (cell_count, tdev, nvar, cells, nf, nb)
     dma = pltpu.SemaphoreType.DMA
@@ -345,8 +346,10 @@
         scratch_shapes=[
             pltpu.VMEM((nvar, 3 * ROWS, cells), BF16),
             pltpu.VMEM((8, 128), F32),
-            pltpu.VMEM((nvar, 2 * tdev, half), F32),
-            pltpu.VMEM((nvar, nf * 2 * kept, half), F32),
+            pltpu.VMEM((nvar, tdev, cells), F32),
+            pltpu.VMEM((nvar, nf * 2 * kept, cells), F32),
+            pltpu.VMEM((nvar, 2 * per, cells), F32),
+            pltpu.VMEM((nvar, 2 * per, cells), F32),
             pltpu.VMEM((2, nvar, per, cells), F32),
             pltpu.VMEM((cells,), F32),
             pltpu.SMEM((nf,), jnp.int32),
@@ -355,8 +358,8 @@
             dma((nvar,)),
             dma((nvar,)),
             dma((nvar,)),
-            dma((3, nvar)),
-            dma((3, nvar)),
+            dma((nvar,)),
+            dma((nvar,)),
             dma((cell_count,)),
             dma((cell_count,)),
             dma((nvar + 1,)),

time: 22.1 us -> 22.3 us (level)
  no operation moved by 1% of the time
where the time goes in v4:
time: 22.3 us; the launch traced here: 22.2 us
  Pallas kernels  21.5 us (96%)
  between operations  0.64 us (3%)
    pallas_call x1, Pallas kernels, on_device(): pl.pallas_call(functools.partial(gather_kernel, sizes), out_shape=(jax.Sh...  18.9 us
    pallas_call x1, Pallas kernels, on_device(): pl.pallas_call(functools.partial(modes_kernel, sizes), out_shape=(jax.Sha...  2.64 us

profile of v4, /device:TPU:0, one launch (start us, length us, event | category | flops | bytes accessed | tf_op | source)
XLA Modules:
  0.0 22.2 jit_solution(8253621861795933694)
XLA Ops:
  0.6 18.9 %shard_map.59 = (bf16[5,96,768]{2,1,0:T(8,128)(2,1)}, f32[8,8,128]{2,1,0:T(8,128)}) custom-call(f32[5,96,768]{2,1,0:T(8,128)} %bitcast.3, f32[768]{0:T(1024)} %vol_hbm.1, s32[8]{0:T(128)} %freq_hbm.1, s32[5]{0:T(128)} %start_hbm.1), custom_call_target="tpu_custom_call" | custom-call | tf_op jit(solution)/shard_map/pallas_call | solution.py:338
  19.5 2.6 %shard_map.60 = (f32[10,5,2,768]{3,2,1,0:T(2,128)}, f32[10,2,10]{2,1,0:T(2,128)}) custom-call(bf16[5,96,768]{2,1,0:T(8,128)(2,1)} %get-tuple-element.6.wcat_hbm, f32[8,8,128]{2,1,0:T(8,128)} %get-tuple-element.7.grams_hbm), custom_call_target="tpu_custom_call" | custom-call | tf_op jit(solution)/shard_map/pallas_call | solution.py:371
